TPU v7x, 512 devices: a whole 4x8x8 slice. The times are simulated.
512 devices in a mesh: fsdp: 32 (over y, x), blk: 16 (over z, core).
Axes of the slice: x: 4, y: 8, z: 8, core: 2. Of those that a mesh axis runs over, the one named last changes fastest.
Arguments:
- out_grad: bfloat16 [6144, 8192], P('fsdp'), may hold values from -6 to 6
- layer_input: bfloat16 [6144, 8192], P('fsdp', 'blk'), may hold values from -6 to 6
- gate_pre: bfloat16 [6144, 14336], P('fsdp', 'blk'), may hold values from -8 to 8
- up_pre: bfloat16 [6144, 14336], P('fsdp', 'blk'), may hold values from -6 to 6
- down_weight: bfloat16 [14336, 8192], P('blk', 'fsdp'), may hold values from -0.0625 to 0.0625
- proj_hidden: bfloat16 [14336, 64], P('blk'), may hold values from -0.046875 to 0.046875
- proj_model: bfloat16 [8192, 128], P('blk'), may hold values from -0.0625 to 0.0625
- example_ids: int32 [32, 192], P('fsdp'), may hold values from 0 to 1, as said below
Outputs:
- down_scores: float32 [64, 8192], P('fsdp', 'blk')
- up_scores: float32 [64, 8192], P('fsdp', 'blk')
Inputs may be any that keep to these rules, and one draw needn't show every extreme that they name: `example_ids`: within each row the example number never falls, and each of the 2 examples holds 48 to 144 neighbouring tokens; in some row one example holds exactly 144.
All inputs are finite; a program needn't handle non-finite values.
Results may differ from a plain program's by a relative error of at most 0.0029.
Values may be sent and summed in bfloat16 or wider, within the bound.
No kernel may reach another device: no remote copies, remote signals or barrier semaphores. Data moves between devices by JAX's collectives and lax.ppermute only.
A program may use at most 64 MiB of HBM per device.

v0:
```python
import jax
import jax.numpy as jnp
from jax import lax
from jax.sharding import PartitionSpec as P

EX_DEV = 2


def per_example(left, right, onehot):
    weighted = onehot[:, :, None] * left[:, None, :]
    scores = jnp.einsum("tek,tm->ekm", weighted, right, precision=lax.Precision.HIGHEST)
    return scores.reshape(onehot.shape[1], left.shape[1] * right.shape[1])


def on_device(
    out_grad, layer_input, gate_pre, up_pre, down_weight, proj_hidden, proj_model, example_ids
):
    blk_index = lax.axis_index("blk")
    feat_width = layer_input.shape[1]
    grad_cols = lax.dynamic_slice_in_dim(out_grad, blk_index * feat_width, feat_width, 1)
    grad_part = jnp.dot(grad_cols, proj_model, preferred_element_type=jnp.float32)
    input_part = jnp.dot(layer_input, proj_model, preferred_element_type=jnp.float32)
    grad_side, input_side = lax.psum((grad_part, input_part), "blk")
    silu_gate = jax.nn.silu(gate_pre.astype(jnp.float32))
    hidden = (silu_gate * up_pre.astype(jnp.float32)).astype(jnp.bfloat16)
    hid_part = jnp.dot(hidden, proj_hidden, preferred_element_type=jnp.float32)
    grad_hidden = lax.dot_general(
        out_grad,
        lax.all_gather(down_weight, "fsdp", axis=1, tiled=True),
        (((1,), (1,)), ((), ())),
        preferred_element_type=jnp.float32,
    )
    grad_up = (grad_hidden * silu_gate).astype(jnp.bfloat16)
    up_part = jnp.dot(grad_up, proj_hidden, preferred_element_type=jnp.float32)
    onehot = (example_ids[0][:, None] == jnp.arange(EX_DEV, dtype=jnp.int32)[None, :]).astype(
        jnp.float32
    )
    down_full = per_example(hid_part, grad_side, onehot)
    up_full = per_example(up_part, input_side, onehot)
    down_scores, up_scores = (
        lax.psum_scatter(down_full, "blk", scatter_dimension=1, tiled=True),
        lax.psum_scatter(up_full, "blk", scatter_dimension=1, tiled=True),
    )
    return (down_scores, up_scores)


def solution(mesh):
    in_specs = (
        P("fsdp", None),
        P("fsdp", "blk"),
        P("fsdp", "blk"),
        P("fsdp", "blk"),
        P("blk", "fsdp"),
        P("blk", None),
        P("blk", None),
        P("fsdp", None),
    )
    out_specs = (P("fsdp", "blk"), P("fsdp", "blk"))
    return jax.shard_map(
        on_device, mesh=mesh, in_specs=in_specs, out_specs=out_specs, check_vma=False
    )
```

profile of v0, /device:TPU:2, one launch (start us, length us, event | category | flops | bytes accessed | tf_op | source)
XLA Modules:
  0.0 275.8 jit_solution(12563792531889700550)
XLA Ops:
  8.0 0.0 copy-start
  8.0 0.0 all-reduce.3.cloned.1.call-start
  8.1 2.0 fusion.21
  10.1 0.0 copy-done
  10.1 1.7 fusion.6
  11.8 0.0 all-reduce.3.cloned.1.call-update
  11.8 0.0 all-gather.2.cloned.1.call-start
  11.9 0.5 all-gather.2.cloned.1.call-update
  12.4 0.0 reduce-scatter.7.cloned.1.call-start
  12.5 0.7 compare_convert_fusion
  13.1 1.5 fusion.5
  14.6 114.8 %all-reduce.3.cloned.1.call-done = (f32[192,128]{1,0:T(8,128)}, f32[192,128]{1,0:T(8,128)}) async-done(((f32[192,128]{1,0:T(8,128)}, f32[192,128]{1,0:T(8,128)}), (f32[192,128]{1,0:T(8,128)}, f32[192,128]{1,0:T(8,128)})) %all-reduce.3.cloned.1.call-update) | async-done | bytes 196624 | tf_op jit(solution)/shard_map/psum | solution.py:23
  129.4 1.2 fusion.10
  130.6 0.0 copy-start.2
  130.6 2.7 copy.14
  133.3 0.0 reduce-scatter.7.cloned.1.call-update
  133.3 0.0 copy-start.1
  133.3 0.0 reduce-scatter.9.cloned.1.call-start
  133.4 28.9 %all-gather.2.cloned.1.call-done = bf16[896,8192]{1,0:T(8,128)(2,1)} async-done(((bf16[896,256]{1,0:T(8,128)(2,1)}), bf16[896,8192]{1,0:T(8,128)(2,1)}) %all-gather.2.cloned.1.call-update) | async-done | bytes 14680080 | tf_op jit(solution)/shard_map/all_gather | solution.py:29
  162.3 0.0 copy-done.2
  162.3 10.5 %fusion.1 = f32[192,64]{0,1:T(8,128)S(1)} fusion(bf16[896,64]{0,1:T(8,128)(2,1)S(1)} %copy-done.2, bf16[192,8192]{1,0:T(8,128)(2,1)S(1)} %copy-done, bf16[896,8192]{1,0:T(8,128)(2,1)} %all-gather.2.cloned.1.call-done, bf16[192,896]{1,0:T(8,128)(2,1)} %param.10), kind=kOutput, calls=%fused_computation.2 | convolution fusion | flops 2841796608 | bytes 18333696 | tf_op jit(solution)/shard_map/dot_general | solution.py:34
  172.8 0.0 copy-done.1
  172.8 0.3 fusion.8
  173.1 2.7 copy.15
  175.8 0.0 reduce-scatter.9.cloned.1.call-update
  175.8 24.2 %reduce-scatter.7.cloned.1.call-done = f32[512,2]{1,0:T(8,128)} async-done(((f32[8192,2]{1,0:T(8,128)}), f32[512,2]{1,0:T(8,128)}) %reduce-scatter.7.cloned.1.call-update) | async-done | bytes 4112
  200.0 1.7 copy.11
  201.6 65.3 %reduce-scatter.9.cloned.1.call-done = f32[512,2]{1,0:T(8,128)} async-done(((f32[8192,2]{1,0:T(8,128)}), f32[512,2]{1,0:T(8,128)}) %reduce-scatter.9.cloned.1.call-update) | async-done | bytes 4112
  267.0 1.7 copy.13
Async XLA Ops:
  8.0 2.1 copy-start
  8.0 121.4 %all-reduce.3.cloned.1.call-start = ((), (), s32[]{:S(2)}) async-start(), calls=%async_computation.5 | async-start | bytes 393216 | tf_op jit(solution)/shard_map/psum | solution.py:23
  11.8 150.5 %all-gather.2.cloned.1.call-start = ((), (), s32[]{:S(2)}) async-start(), calls=%async_computation.2 | async-start | bytes 15138816 | tf_op jit(solution)/shard_map/all_gather | solution.py:29
  12.4 187.6 %reduce-scatter.7.cloned.1.call-start = ((), (), s32[]{:S(2)}) async-start(), calls=%async_computation.3 | async-start | bytes 4456448
  130.6 31.7 %copy-start.2 = (bf16[896,64]{0,1:T(8,128)(2,1)S(1)}, bf16[896,64]{0,1:T(8,128)(2,1)}, u32[]{:S(2)}) copy-start(bf16[896,64]{0,1:T(8,128)(2,1)} %param.13) | copy-start | bytes 344068
  133.3 39.5 %copy-start.1 = (f32[192,128]{1,0:T(8,128)S(1)}, f32[192,128]{1,0:T(8,128)}, u32[]{:S(2)}) copy-start(f32[192,128]{1,0:T(8,128)} %get-tuple-element.3) | copy-start | bytes 294916
  133.3 133.7 %reduce-scatter.9.cloned.1.call-start = ((), (), s32[]{:S(2)}) async-start(), calls=%async_computation.4 | async-start | bytes 4456448
Sparse Core Ops, SparseCore 0:
  12.0 117.4 all-reduce.2
  133.4 66.5 reduce-scatter.6
  203.1 63.8 reduce-scatter.8
Sparse Core Ops, SparseCore 1:
  15.8 146.4 all-gather.1
where the time goes:
time: 276 us
  waiting for transfers between devices  234 us (85%)
  matrix products  17.2 us (6%)
  between operations  15.3 us (6%)
  local copies, waits for them, and re-layouts  8.68 us (3%)
    psum x1, waiting for transfers between devices, on_device(): grad_side, input_side = lax.psum((grad_part, input_part), 'blk')  115 us
    unnamed x6, waiting for transfers between devices  90.1 us
    all_gather x1, waiting for transfers between devices, on_device(): lax.all_gather(down_weight, 'fsdp', axis=1, tiled=True)  28.9 us
    dot_general x1, matrix products, on_device(): up_part = jnp.dot(grad_up, proj_hidden, preferred_element_type=jnp.float32)  10.5 us
    unnamed x10, local copies, waits for them, and re-layouts  8.68 us
  transfers between devices with their start and end apart: 4, of which 4 were waited for; matrix products, arithmetic and copies ran while one was open for 8% of the time, Pallas kernels for 0%

commit v1 on v0

--- a/solution.py
+++ b/solution.py
@@ -26,7 +26,9 @@
     hid_part = jnp.dot(hidden, proj_hidden, preferred_element_type=jnp.float32)
     grad_hidden = lax.dot_general(
         out_grad,
-        lax.all_gather(down_weight, "fsdp", axis=1, tiled=True),
+        jnp.concatenate(
+            lax.all_to_all(jnp.stack([down_weight] * lax.axis_size("fsdp")), "fsdp", 0, 0), axis=1
+        ),
         (((1,), (1,)), ((), ())),
         preferred_element_type=jnp.float32,
     )

time: 276 us -> 476 us (1.72)
  the two profiles are of different devices: /device:TPU:2 before, /device:TPU:12 now
where the time goes in v1:
time: 476 us; the launch traced here: 475 us
  waiting for transfers between devices  418 us (88%)
  local copies, waits for them, and re-layouts  19.1 us (4%)
  between operations  13.9 us (3%)
  matrix products  13.4 us (3%)
  starting transfers between devices  10.8 us (2%)
    all_to_all x1, waiting for transfers between devices, on_device(): lax.all_to_all(jnp.stack([down_weight] * lax.axis_size('fsdp')), 'fsdp',...  204 us
    psum x1, waiting for transfers between devices, on_device(): grad_side, input_side = lax.psum((grad_part, input_part), 'blk')  118 us
    unnamed x5, waiting for transfers between devices  96.6 us
    unnamed x17, local copies, waits for them, and re-layouts  10.7 us
    all_to_all x1, starting transfers between devices, on_device(): lax.all_to_all(jnp.stack([down_weight] * lax.axis_size('fsdp')), 'fsdp',...  10.6 us
  transfers between devices with their start and end apart: 4, of which 3 were waited for; matrix products, arithmetic and copies ran while one was open for 4% of the time, Pallas kernels for 0%

profile of v1, /device:TPU:12, one launch (start us, length us, event | category | flops | bytes accessed | tf_op | source)
XLA Modules:
  0.0 475.4 jit_solution(6478904892759960711)
XLA Ops:
  7.2 0.0 copy-start
  7.2 2.2 copy.11
  9.3 8.3 %stack.2 = bf16[32,896,256]{1,2,0:T(8,128)(2,1)} broadcast(bf16[896,256]{0,1:T(8,128)(2,1)} %copy.11), dimensions={1,2} | broadcast | bytes 15138816 | tf_op jit(solution)/shard_map/stack | solution.py:30
  17.6 0.0 copy-start.1
  17.6 0.0 copy-start.2
  17.6 10.6 %all-to-all-start = ((bf16[32,896,256]{1,2,0:T(8,128)(2,1)}), bf16[32,896,256]{1,2,0:T(8,128)(2,1)}, u32[]{:S(2)}, u32[]{:S(2)}) async-start(bf16[32,896,256]{1,2,0:T(8,128)(2,1)} %stack.2), calls=%async_computation | async-start | bytes 29360128 | tf_op jit(solution)/shard_map/all_to_all | solution.py:30
  28.3 0.0 copy-start.4
  28.3 0.0 all-reduce.3.cloned.1.call-start
  28.4 0.0 copy-done
  28.4 0.0 copy-done.1
  28.4 0.8 fusion.6
  29.2 0.0 copy-done.2
  29.2 0.8 fusion.21
  30.1 0.0 all-reduce.3.cloned.1.call-update
  30.1 0.0 reduce-scatter.7.cloned.1.call-start
  30.1 1.5 fusion.5
  31.6 0.0 copy-done.4
  31.6 117.6 %all-reduce.3.cloned.1.call-done = (f32[192,128]{1,0:T(8,128)}, f32[192,128]{1,0:T(8,128)}) async-done(((f32[192,128]{1,0:T(8,128)}, f32[192,128]{1,0:T(8,128)}), (f32[192,128]{1,0:T(8,128)}, f32[192,128]{1,0:T(8,128)})) %all-reduce.3.cloned.1.call-update) | async-done | bytes 196624 | tf_op jit(solution)/shard_map/psum | solution.py:23
  149.2 1.2 fusion.10
  150.4 0.0 copy-start.5
  150.4 2.6 copy.16
  153.0 0.0 reduce-scatter.7.cloned.1.call-update
  153.0 0.0 reduce-scatter.9.cloned.1.call-start
  153.1 204.2 %all-to-all-done = bf16[32,896,256]{1,2,0:T(8,128)(2,1)} async-done(((bf16[32,896,256]{1,2,0:T(8,128)(2,1)}), bf16[32,896,256]{1,2,0:T(8,128)(2,1)}, u32[]{:S(2)}, u32[]{:S(2)}) %all-to-all-start) | async-done | bytes 14680096 | tf_op jit(solution)/shard_map/all_to_all | solution.py:30
  357.3 0.0 copy-done.5
  357.3 0.0 copy-start.3
  357.3 8.8 %fusion.1 = f32[192,64]{0,1:T(8,128)S(1)} fusion(bf16[896,64]{0,1:T(8,128)(2,1)S(1)} %copy-done.5, bf16[192,8192]{1,0:T(8,128)(2,1)S(1)} %copy-done, bf16[896,8192]{0,1:T(8,128)(2,1)} %bitcast.3, bf16[192,896]{1,0:T(8,128)(2,1)} %param.10), kind=kOutput, calls=%fused_computation.2 | convolution fusion | flops 2841796608 | bytes 18333696 | tf_op jit(solution)/shard_map/dot_general | solution.py:36
  366.1 0.0 copy-done.3
  366.1 0.3 fusion.8
  366.4 2.6 copy.17
  369.0 0.0 reduce-scatter.9.cloned.1.call-update
  369.0 0.0 reduce-scatter.7.cloned.1.call-done
  369.1 1.7 copy.13
  370.7 96.5 %reduce-scatter.9.cloned.1.call-done = f32[512,2]{1,0:T(8,128)} async-done(((f32[8192,2]{1,0:T(8,128)}), f32[512,2]{1,0:T(8,128)}) %reduce-scatter.9.cloned.1.call-update) | async-done | bytes 4112
  467.3 1.7 copy.15
  (1 shorter events, 0.0 us)
Async XLA Ops:
  7.2 21.2 %copy-start = (bf16[192,8192]{1,0:T(8,128)(2,1)S(1)}, bf16[192,8192]{1,0:T(8,128)(2,1)}, u32[]{:S(2)}) copy-start(bf16[192,8192]{1,0:T(8,128)(2,1)} %param.8) | copy-start | bytes 9437188
  17.6 10.7 %copy-start.1 = (bf16[512,128]{1,0:T(8,128)(2,1)S(1)}, bf16[512,128]{1,0:T(8,128)(2,1)}, u32[]{:S(2)}) copy-start(bf16[512,128]{1,0:T(8,128)(2,1)} %param.14) | copy-start | bytes 393220
  17.6 11.6 %copy-start.2 = (bf16[192,512]{1,0:T(8,128)(2,1)S(1)}, bf16[192,512]{1,0:T(8,128)(2,1)}, u32[]{:S(2)}) copy-start(bf16[192,512]{1,0:T(8,128)(2,1)} %param.9) | copy-start | bytes 589828
  17.6 339.6 %all-to-all-start = ((bf16[32,896,256]{1,2,0:T(8,128)(2,1)}), bf16[32,896,256]{1,2,0:T(8,128)(2,1)}, u32[]{:S(2)}, u32[]{:S(2)}) async-start(bf16[32,896,256]{1,2,0:T(8,128)(2,1)} %stack.2), calls=%async_computation | async-start | bytes 29360128 | tf_op jit(solution)/shard_map/all_to_all | solution.py:30
  28.3 3.3 copy-start.4
  28.3 120.9 %all-reduce.3.cloned.1.call-start = ((), (), s32[]{:S(2)}) async-start(), calls=%async_computation.5 | async-start | bytes 393216 | tf_op jit(solution)/shard_map/psum | solution.py:23
  30.1 339.0 %reduce-scatter.7.cloned.1.call-start = ((), (), s32[]{:S(2)}) async-start(), calls=%async_computation.3 | async-start | bytes 4456448
  150.4 206.9 %copy-start.5 = (bf16[896,64]{0,1:T(8,128)(2,1)S(1)}, bf16[896,64]{0,1:T(8,128)(2,1)}, u32[]{:S(2)}) copy-start(bf16[896,64]{0,1:T(8,128)(2,1)} %param.13) | copy-start | bytes 344068
  153.0 314.2 %reduce-scatter.9.cloned.1.call-start = ((), (), s32[]{:S(2)}) async-start(), calls=%async_computation.4 | async-start | bytes 4456448
  357.3 8.8 %copy-start.3 = (f32[192,128]{1,0:T(8,128)S(1)}, f32[192,128]{1,0:T(8,128)}, u32[]{:S(2)}) copy-start(f32[192,128]{1,0:T(8,128)} %get-tuple-element.3) | copy-start | bytes 294916
Sparse Core Ops, SparseCore 0:
  31.6 117.6 all-reduce.2
  153.2 68.3 reduce-scatter.6
  369.2 98.0 reduce-scatter.8
